TPU v7x, 32 devices: a whole 2x2x4 slice. The times are simulated.
32 devices in a mesh: groups: 2 (over x), dp: 8 (over z, y), own: 2 (over core).
Axes of the slice: x: 2, y: 2, z: 4, core: 2. Of those that a mesh axis runs over, the one named last changes fastest.
Arguments:
- acts: bfloat16 [2048, 8192], P(('groups', 'dp')), parts along dimension 0, may hold values from -6 to 6
- grad_out: bfloat16 [2048, 8192], P(('groups', 'dp')), parts along dimension 0, may hold values from -6 to 6
- weight_blocks: bfloat16 [1664, 4096], P(('dp', 'own')), may hold values from -0.21875 to 0.21875
- block_rows: int32 [1664], replicated, may hold values from 0 to 127, as said below
- block_cols: int32 [1664], replicated, may hold values from 0 to 127, as said below
Outputs:
- grad_blocks: bfloat16 [3328, 4096], P(('groups', 'dp', 'own')), parts along dimension 0
- grad_acts: bfloat16 [2048, 8192], P(('groups', 'dp'), 'own'), parts along dimension 0
There are 2 independent parts, one for each index of `groups`. A program takes and returns all parts, laid end to end along the dimension named above; an argument that names none is the same for every part. Nothing has to cross between parts.
Inputs may be any that keep to these rules, and one draw needn't show every extreme that they name: `block_rows`: together with block_cols at the same index it names one block of the 128 x 8192/64 grid of blocks; no block is named twice; block (0, 0) and the last block of the grid are always named. `block_cols`: see block_rows.
All inputs are finite; a program needn't handle non-finite values.
Results may differ from a plain program's by a relative error of at most 0.001.
Values may be sent and summed in bfloat16 or wider, within the bound.
A program may use at most 128 MiB of HBM per device.

v0:
```python
import math

import jax
import jax.numpy as jnp
from jax import lax
from jax.sharding import PartitionSpec as P

BLOCK = 64


def per_device(acts, grad_out, weight_blocks, block_rows, block_cols):
    tok_rows = acts.shape[0]
    feature_width = acts.shape[1]
    row_blocks = feature_width // BLOCK
    n_data = lax.axis_size("dp")
    n_owners = lax.axis_size("own")
    own_index = lax.axis_index("own")
    local_blocks = weight_blocks.shape[0]
    half_count = n_data * local_blocks
    slot_ids = jnp.arange(half_count, dtype=jnp.int32)
    global_ids = (
        slot_ids // local_blocks * n_owners + own_index
    ) * local_blocks + slot_ids % local_blocks
    half_rows = block_rows[global_ids]
    half_cols = block_cols[global_ids]
    grad_scale = 1.0 / math.sqrt(tok_rows * n_data)
    acts_three = acts.reshape(tok_rows, row_blocks, BLOCK)
    grad_three = grad_out.reshape(tok_rows, row_blocks, BLOCK)
    rows_here = half_rows.reshape(-1, local_blocks)
    cols_here = half_cols.reshape(-1, local_blocks)

    def one_group(pair):
        left = acts_three[:, pair[0]]
        right = grad_three[:, pair[1]]
        product = jnp.einsum("tbi,tbj->bij", left, right, preferred_element_type=jnp.float32)
        return product.reshape(local_blocks, BLOCK * BLOCK)

    grouped = lax.map(one_group, (rows_here, cols_here))
    block_totals = lax.psum_scatter(
        grouped.reshape(half_count, BLOCK * BLOCK) * grad_scale,
        "dp",
        scatter_dimension=0,
        tiled=True,
    )
    grad_blocks = block_totals.astype(jnp.bfloat16)
    start_totals = jnp.zeros((tok_rows, row_blocks, BLOCK), jnp.float32)
    all_weights = lax.all_gather(weight_blocks, "dp", axis=0, tiled=True)
    amount = all_weights.shape[0]

    def one_step(group_idx, running):
        offset = group_idx * local_blocks
        sub_piece = lax.dynamic_slice_in_dim(all_weights, offset, local_blocks, 0)
        rows_here = lax.dynamic_slice_in_dim(half_rows, 0 + offset, local_blocks)
        cols_here = lax.dynamic_slice_in_dim(half_cols, 0 + offset, local_blocks)
        weights_here = sub_piece.reshape(local_blocks, BLOCK, BLOCK)
        right = grad_three[:, cols_here]
        contrib = jnp.einsum(
            "tbj,bij->tbi", right, weights_here, preferred_element_type=jnp.float32
        )
        return running.at[:, rows_here].add(contrib)

    totals = lax.fori_loop(0, amount // local_blocks, one_step, start_totals)
    partial_grad = totals.reshape(tok_rows, feature_width)
    grad_acts = lax.psum_scatter(partial_grad, "own", scatter_dimension=1, tiled=True).astype(
        jnp.bfloat16
    )
    return (grad_blocks, grad_acts)


def solution(mesh):
    in_specs = (
        P(("groups", "dp"), None),
        P(("groups", "dp"), None),
        P(("dp", "own"), None),
        P(),
        P(),
    )
    out_specs = (P(("groups", "dp", "own"), None), P(("groups", "dp"), "own"))
    return jax.shard_map(
        per_device, mesh=mesh, in_specs=in_specs, out_specs=out_specs, check_vma=False
    )
```

profile of v0, /device:TPU:9, one launch (start us, length us, event | category | flops | bytes accessed | tf_op | source)
XLA Modules:
  0.0 765.2 jit_solution(5427068931238185959)
XLA Ops:
  8.1 4.9 gather_fusion.3
  13.0 4.9 gather_fusion.4
  21.3 4.2 copy.20
  25.5 89.2 %all-gather.2.cloned.1.call-done = bf16[832,4096]{1,0:T(8,128)(2,1)} async-done(((bf16[104,4096]{1,0:T(8,128)(2,1)}), bf16[832,4096]{1,0:T(8,128)(2,1)}) %all-gather.2.cloned.1.call-update) | async-done | bytes 6815760 | tf_op jit(solution)/shard_map/all_gather | solution.py:47
  117.3 248.6 %while.24 = (s32[]{:T(128)}, f32[128,128,64]{0,2,1:T(8,128)}, s32[832]{0:T(1024)S(1)}, bf16[832,4096]{1,0:T(8,128)(2,1)}, s32[832]{0:T(1024)S(1)}, /*index=5*/bf...) while((s32[]{:T(128)}, f32[128,128,64]{0,2,1:T(8,128)}, s32[832]{0:T(1024)S(1)}, ...), condition=%wide.region_5.6_spmd, body=%wide.region_3.5_spmd.sunk | while | flops 109905528 | bytes 24714236 | solution.py:62
  126.3 4.3 fusion.28
  130.7 17.7 %scatter_fusion = f32[128,128,64]{0,2,1:T(8,128)} fusion(f32[128,128,64]{0,2,1:T(8,128)} %get-tuple-element.297, s32[104]{0:T(128)S(1)} %get-tuple-element.263, f32[104,128,64]{1,2,0:T(8,128)} %fusion.28), kind=kCustom, calls=%fused_computation.5.clone.1 | custom fusion | flops 851968 | bytes 10224032 | tf_op jit(solution)/shard_map/while/body/eval_jaxpr/scatter-add | solution.py:60
  157.4 4.3 fusion.28
  161.7 17.7 %scatter_fusion = f32[128,128,64]{0,2,1:T(8,128)} fusion(f32[128,128,64]{0,2,1:T(8,128)} %get-tuple-element.297, s32[104]{0:T(128)S(1)} %get-tuple-element.263, f32[104,128,64]{1,2,0:T(8,128)} %fusion.28), kind=kCustom, calls=%fused_computation.5.clone.1 | custom fusion | flops 851968 | bytes 10224032 | tf_op jit(solution)/shard_map/while/body/eval_jaxpr/scatter-add | solution.py:60
  188.4 4.3 fusion.28
  192.8 17.6 %scatter_fusion = f32[128,128,64]{0,2,1:T(8,128)} fusion(f32[128,128,64]{0,2,1:T(8,128)} %get-tuple-element.297, s32[104]{0:T(128)S(1)} %get-tuple-element.263, f32[104,128,64]{1,2,0:T(8,128)} %fusion.28), kind=kCustom, calls=%fused_computation.5.clone.1 | custom fusion | flops 851968 | bytes 10224032 | tf_op jit(solution)/shard_map/while/body/eval_jaxpr/scatter-add | solution.py:60
  219.5 4.3 fusion.28
  223.8 17.6 %scatter_fusion = f32[128,128,64]{0,2,1:T(8,128)} fusion(f32[128,128,64]{0,2,1:T(8,128)} %get-tuple-element.297, s32[104]{0:T(128)S(1)} %get-tuple-element.263, f32[104,128,64]{1,2,0:T(8,128)} %fusion.28), kind=kCustom, calls=%fused_computation.5.clone.1 | custom fusion | flops 851968 | bytes 10224032 | tf_op jit(solution)/shard_map/while/body/eval_jaxpr/scatter-add | solution.py:60
  250.5 4.3 fusion.28
  254.9 17.6 %scatter_fusion = f32[128,128,64]{0,2,1:T(8,128)} fusion(f32[128,128,64]{0,2,1:T(8,128)} %get-tuple-element.297, s32[104]{0:T(128)S(1)} %get-tuple-element.263, f32[104,128,64]{1,2,0:T(8,128)} %fusion.28), kind=kCustom, calls=%fused_computation.5.clone.1 | custom fusion | flops 851968 | bytes 10224032 | tf_op jit(solution)/shard_map/while/body/eval_jaxpr/scatter-add | solution.py:60
  281.5 4.3 fusion.28
  285.9 17.7 %scatter_fusion = f32[128,128,64]{0,2,1:T(8,128)} fusion(f32[128,128,64]{0,2,1:T(8,128)} %get-tuple-element.297, s32[104]{0:T(128)S(1)} %get-tuple-element.263, f32[104,128,64]{1,2,0:T(8,128)} %fusion.28), kind=kCustom, calls=%fused_computation.5.clone.1 | custom fusion | flops 851968 | bytes 10224032 | tf_op jit(solution)/shard_map/while/body/eval_jaxpr/scatter-add | solution.py:60
  312.6 4.4 fusion.28
  316.9 17.7 %scatter_fusion = f32[128,128,64]{0,2,1:T(8,128)} fusion(f32[128,128,64]{0,2,1:T(8,128)} %get-tuple-element.297, s32[104]{0:T(128)S(1)} %get-tuple-element.263, f32[104,128,64]{1,2,0:T(8,128)} %fusion.28), kind=kCustom, calls=%fused_computation.5.clone.1 | custom fusion | flops 851968 | bytes 10224032 | tf_op jit(solution)/shard_map/while/body/eval_jaxpr/scatter-add | solution.py:60
  343.7 4.3 fusion.28
  348.0 17.9 %scatter_fusion = f32[128,128,64]{0,2,1:T(8,128)} fusion(f32[128,128,64]{0,2,1:T(8,128)} %get-tuple-element.297, s32[104]{0:T(128)S(1)} %get-tuple-element.263, f32[104,128,64]{1,2,0:T(8,128)} %fusion.28), kind=kCustom, calls=%fused_computation.5.clone.1 | custom fusion | flops 851968 | bytes 10224032 | tf_op jit(solution)/shard_map/while/body/eval_jaxpr/scatter-add | solution.py:60
  366.0 142.2 %while.23 = (s32[]{:T(128)}, f32[8,104,4096]{1,2,0:T(8,128)}, s32[8,104]{1,0:T(8,128)S(1)}, bf16[128,128,64]{0,2,1:T(8,128)(2,1)}, s32[8,104]{1,0:T(8,128)S(1)}, /*index=5*/bf16[128,128,64]{0,2,1:T(8,128)(2,1)S(1)}, s32[]{:T(128)}) while((s32[]{:T(128)}, f32[8,104,4096]{1,2,0:T(8,128)}, s32[8,104]{1,0:T(8,128)S(1)}, ...), condition=%wide.region_1.2_spmd, body=%wide.region_0.1_spmd.sunk | while | flops 109054576 | bytes 19541840 | solution.py:38
  368.1 3.6 gather_fusion.1
  371.7 5.5 fusion.25
  377.2 4.3 copy.29
  386.6 3.6 gather_fusion.1
  390.2 4.7 fusion.25
  394.9 4.2 copy.29
  404.3 3.6 gather_fusion.1
  407.8 4.7 fusion.25
  412.6 4.2 copy.29
  421.9 3.6 gather_fusion.1
  425.5 4.7 fusion.25
  430.2 4.2 copy.29
  439.6 3.6 gather_fusion.1
  443.2 4.7 fusion.25
  447.9 4.2 copy.29
  457.3 3.6 gather_fusion.1
  460.9 4.7 fusion.25
  465.6 4.2 copy.29
  475.0 3.6 gather_fusion.1
  478.5 4.7 fusion.25
  483.3 4.2 copy.29
  496.2 4.7 fusion.25
  500.9 4.2 copy.29
  508.2 11.2 %broadcast_multiply_fusion = f32[8,104,4096]{1,2,0:T(8,128)} fusion(f32[8,104,4096]{1,2,0:T(8,128)} %get-tuple-element.143), kind=kLoop, calls=%fused_computation.26 | loop fusion | flops 3407872 | bytes 27262976 | tf_op jit(solution)/shard_map/mul | solution.py:40
  519.4 16.6 %copy.22 = f32[8,104,4096]{2,1,0:T(8,128)} copy(f32[8,104,4096]{1,2,0:T(8,128)} %broadcast_multiply_fusion) | data formatting | bytes 27262976 | tf_op jit(solution)/shard_map/mul | solution.py:40
  539.1 217.1 %reduce-scatter.3.cloned.1.call-done = f32[104,4096]{1,0:T(8,128)} async-done(((f32[832,4096]{1,0:T(8,128)}), f32[104,4096]{1,0:T(8,128)}) %reduce-scatter.3.cloned.1.call-update) | async-done | bytes 1703952 | tf_op jit(solution)/shard_map/reduce_scatter | solution.py:39
  (112 shorter events, 129.4 us)
Async XLA Ops:
  7.2 0.9 copy-start
  7.2 5.8 copy-start.2
  7.2 107.5 %all-gather.2.cloned.1.call-start = ((), (), s32[]{:S(2)}) async-start(), calls=%async_computation.3 | async-start | bytes 7667712 | tf_op jit(solution)/shard_map/all_gather | solution.py:47
  7.9 528.1 %reduce-scatter.5.cloned.1.call-start = ((), (), s32[]{:S(2)}) async-start(), calls=%async_computation.4 | async-start | bytes 6291456 | tf_op jit(solution)/shard_map/reduce_scatter | solution.py:64
  365.9 390.3 %reduce-scatter.3.cloned.1.call-start = ((), (), s32[]{:S(2)}) async-start(), calls=%async_computation.2 | async-start | bytes 15335424 | tf_op jit(solution)/shard_map/reduce_scatter | solution.py:39
  536.0 222.6 %copy-start.1 = (s32[1664]{0:T(1024)S(1)}, s32[1664]{0:T(1024)}, u32[]{:S(2)}) copy-start(s32[1664]{0:T(1024)} %param.12) | copy-start | bytes 19972
Sparse Core Ops, SparseCore 0:
  10.2 104.4 all-gather.1
  366.0 13.1 reduce-scatter.4
  536.1 220.0 reduce-scatter.2
where the time goes:
time: 772 us; the launch traced here: 765 us
  waiting for transfers between devices  307 us (40%)
  local copies, waits for them, and re-layouts  213 us (28%)
  other arithmetic  158 us (20%)
  matrix products  73.3 us (9%)
  between operations  13.8 us (2%)
    reduce_scatter x1, waiting for transfers between devices, per_device(): lax.psum_scatter(grouped.reshape(half_count, BLOCK * BLOCK) * grad_scale,...  217 us
    scatter-add x8, other arithmetic, one_step(): return running.at[:, rows_here].add(contrib)  141 us
    all_gather x1, waiting for transfers between devices, per_device(): all_weights = lax.all_gather(weight_blocks, 'dp', axis=0, tiled=True)  89.2 us
    dot_general x8, matrix products, one_group(): jnp.einsum('tbi,tbj->bij', left, right, preferred_element_type=jnp.float32)  38.5 us
    dot_general x8, matrix products, one_step(): jnp.einsum('tbj,bij->tbi', right, weights_here, preferred_element_type=jn...  34.8 us
    dot_general x8, local copies, waits for them, and re-layouts, one_group(): jnp.einsum('tbi,tbj->bij', left, right, preferred_element_type=jnp.float32)  33.9 us
    dynamic_slice x16, local copies, waits for them, and re-layouts, one_step(): sub_piece = lax.dynamic_slice_in_dim(all_weights, offset, local_blocks, 0)  29.6 us
    gather x8, local copies, waits for them, and re-layouts, one_group(): left = acts_three[:, pair[0]]  28.6 us
  transfers between devices with their start and end apart: 3, of which 2 were waited for; matrix products, arithmetic and copies ran while one was open for 25% of the time, Pallas kernels for 0%

commit v1 on v0

v1 whole, which is shorter than its diff:
```python
import functools
import math

import jax
import jax.numpy as jnp
from jax import lax
from jax.experimental import pallas as pl
from jax.experimental.pallas import tpu as pltpu
from jax.sharding import PartitionSpec as P

BLOCK = 64
LANES = 2 * BLOCK
MIB = 1024 * 1024


def block_grad_kernel(scale, rows_ref, cols_ref, a0, a1, g0, g1, out_ref):
    pairs = out_ref.shape[0]
    start = pl.program_id(0) * pairs
    left_half = lax.broadcasted_iota(jnp.int32, (BLOCK, LANES), 1) < BLOCK

    def features(ref, other, at):
        rows = pl.ds(pl.multiple_of(at * BLOCK, BLOCK), BLOCK)
        return jnp.concatenate([ref[rows, :], other[rows, :]], axis=1)

    def one_pair(p, carry):
        b = 2 * (start + p)
        lhs = jnp.concatenate([features(a0, a1, rows_ref[b + k]) for k in range(2)], axis=0)
        rhs = jnp.concatenate([features(g0, g1, cols_ref[b + k]) for k in range(2)], axis=0)
        prod = lax.dot_general(
            lhs, rhs, (((1,), (1,)), ((), ())), preferred_element_type=jnp.float32
        )
        out_ref[p] = jnp.where(left_half, prod[:BLOCK], prod[BLOCK:]) * scale
        return carry

    lax.fori_loop(0, pairs, one_pair, 0, unroll=4)


def block_grads(rows, cols, a0, a1, g0, g1, scale, steps):
    pairs = rows.shape[0] // 2
    whole = pl.BlockSpec(a0.shape, lambda i, *_: (0, 0))
    return pl.pallas_call(
        functools.partial(block_grad_kernel, scale),
        out_shape=jax.ShapeDtypeStruct((pairs, BLOCK, LANES), jnp.float32),
        grid_spec=pltpu.PrefetchScalarGridSpec(
            num_scalar_prefetch=2,
            grid=(steps,),
            in_specs=[whole] * 4,
            out_specs=pl.BlockSpec((pairs // steps, BLOCK, LANES), lambda i, *_: (i, 0, 0)),
        ),
        compiler_params=pltpu.CompilerParams(vmem_limit_bytes=48 * MIB),
        cost_estimate=pl.CostEstimate(
            flops=pairs * 2 * LANES * LANES * 512, bytes_accessed=16 * MIB, transcendentals=0
        ),
        name="block_grads",
    )(rows, cols, a0, a1, g0, g1)


def input_grad_kernel(rows_ref, cols_ref, w_ref, g_ref, out_ref):
    pairs = w_ref.shape[0]
    start = pl.program_id(0) * pairs
    lane = lax.broadcasted_iota(jnp.int32, (BLOCK, LANES), 1)
    first = (lane < BLOCK).astype(jnp.float32).astype(jnp.bfloat16)
    second = (lane >= BLOCK).astype(jnp.float32).astype(jnp.bfloat16)

    @pl.when(pl.program_id(0) == 0)
    def _():
        out_ref[...] = jnp.zeros_like(out_ref)

    def span(at):
        return pl.ds(pl.multiple_of(at * BLOCK, BLOCK), BLOCK)

    def one_pair(p, carry):
        b = 2 * (start + p)
        w = w_ref[p]
        lhs = jnp.concatenate([w * first, w * second], axis=0)
        rhs = jnp.concatenate([g_ref[span(cols_ref[b + k]), :] for k in range(2)], axis=0)
        prod = jnp.dot(lhs, rhs, preferred_element_type=jnp.float32)
        for k in range(2):
            out_ref[span(rows_ref[b + k]), :] += prod[k * BLOCK : (k + 1) * BLOCK]
        return carry

    lax.fori_loop(0, pairs, one_pair, 0, unroll=4)


def input_grad(rows, cols, weights, g, steps):
    pairs = weights.shape[0]
    return pl.pallas_call(
        input_grad_kernel,
        out_shape=jax.ShapeDtypeStruct(g.shape, jnp.float32),
        grid_spec=pltpu.PrefetchScalarGridSpec(
            num_scalar_prefetch=2,
            grid=(steps,),
            in_specs=[
                pl.BlockSpec((pairs // steps, BLOCK, LANES), lambda i, *_: (i, 0, 0)),
                pl.BlockSpec(g.shape, lambda i, *_: (0, 0)),
            ],
            out_specs=pl.BlockSpec(g.shape, lambda i, *_: (0, 0)),
        ),
        compiler_params=pltpu.CompilerParams(vmem_limit_bytes=48 * MIB),
        cost_estimate=pl.CostEstimate(
            flops=pairs * 2 * LANES * LANES * 1024, bytes_accessed=13 * MIB, transcendentals=0
        ),
        name="input_grad",
    )(rows, cols, weights, g)


def per_device(acts, grad_out, weight_blocks, block_rows, block_cols):
    tok_rows, width = acts.shape
    n_data = lax.axis_size("dp")
    data_index = lax.axis_index("dp")
    own_index = lax.axis_index("own")
    local_blocks = weight_blocks.shape[0]
    scale = 1.0 / math.sqrt(tok_rows * n_data)

    w_pairs = (
        weight_blocks.reshape(local_blocks // 2, 2, BLOCK, BLOCK)
        .transpose(0, 2, 1, 3)
        .reshape(local_blocks // 2, BLOCK, LANES)
    )
    all_weights = lax.all_gather(w_pairs, "dp", axis=0, tiled=True)

    half = width // 2
    both = jnp.stack([acts, grad_out])
    both_half = lax.dynamic_slice_in_dim(both, own_index * half, half, axis=2)
    mine_t = both.transpose(0, 2, 1)
    half_t = both_half.transpose(0, 2, 1)
    swap = [(d, d ^ 1) for d in range(n_data)]
    came = lax.ppermute(half_t, "dp", swap)
    pair_t = lax.all_gather(came, "own", axis=1, tiled=True)

    by_owner_rows = block_rows.reshape(n_data // 2, 2, 2, local_blocks)
    by_owner_cols = block_cols.reshape(n_data // 2, 2, 2, local_blocks)
    half_rows = by_owner_rows[:, :, own_index]
    half_cols = by_owner_cols[:, :, own_index]
    sub_rows = half_rows[:, data_index % 2].reshape(-1)
    sub_cols = half_cols[:, data_index % 2].reshape(-1)

    partial = block_grads(
        sub_rows, sub_cols, mine_t[0], pair_t[0], mine_t[1], pair_t[1], scale, 4
    )
    later_rows, partial = lax.optimization_barrier((half_rows.reshape(-1), partial))
    groups = [list(range(k, n_data, 2)) for k in range(2)]
    summed = lax.psum_scatter(
        partial, "dp", scatter_dimension=0, axis_index_groups=groups, tiled=True
    )
    grad_blocks = (
        summed.astype(jnp.bfloat16)
        .reshape(local_blocks // 2, BLOCK, 2, BLOCK)
        .transpose(0, 2, 1, 3)
        .reshape(local_blocks, BLOCK * BLOCK)
    )

    total_t = input_grad(later_rows, half_cols.reshape(-1), all_weights, mine_t[1], 8)
    ga_t = lax.psum_scatter(total_t, "own", scatter_dimension=0, tiled=True)
    grad_acts = ga_t.astype(jnp.bfloat16).T
    return (grad_blocks, grad_acts)


def solution(mesh):
    in_specs = (
        P(("groups", "dp"), None),
        P(("groups", "dp"), None),
        P(("dp", "own"), None),
        P(),
        P(),
    )
    out_specs = (P(("groups", "dp", "own"), None), P(("groups", "dp"), "own"))
    return jax.shard_map(
        per_device, mesh=mesh, in_specs=in_specs, out_specs=out_specs, check_vma=False
    )
```

time: 772 us -> 334 us (0.43)
  local copies, waits for them, and re-layouts: 213 us -> 32.2 us
  other arithmetic: 158 us -> 6.77 us
  matrix products: 73.3 us -> 0 us
  waiting for transfers between devices: 307 us -> 238 us
  Pallas kernels: 0 us -> 40.8 us
    scatter-add x8 -> x0, other arithmetic: 141 us -> none  [one_step(): return running.at[:, rows_here].add(contrib)]
    reduce_scatter x2, waiting for transfers between devices: 217 us -> 106 us  [the longest x1 97.8 us: per_device(): lax.psum_scatter(partial, 'dp', scatter_dimension=0, axis_index_groups=gr...]
    dot_general x16 -> x0, matrix products: 73.3 us -> none  [the longest x8 38.5 us: one_group(): jnp.einsum('tbi,tbj->bij', left, right, preferred_element_type=jnp.float32)]
    gather x26 -> x0, local copies, waits for them, and re-layouts: 70.8 us -> none  [the longest x8 28.6 us: one_group(): left = acts_three[:, pair[0]]]
    ppermute x0 -> x1, waiting for transfers between devices: none -> 45.4 us  [per_device(): came = lax.ppermute(half_t, 'dp', swap)]
    pallas_call x0 -> x2, Pallas kernels: none -> 40.8 us  [the longest x1 24.3 us: input_grad(): pl.pallas_call(input_grad_kernel, out_shape=jax.ShapeDtypeStruct(g.shape,...]
    dot_general x8 -> x0, local copies, waits for them, and re-layouts: 33.9 us -> none  [one_group(): jnp.einsum('tbi,tbj->bij', left, right, preferred_element_type=jnp.float32)]
    dynamic_slice x16 -> x3, local copies, waits for them, and re-layouts: 29.6 us -> 0.08 us  [the longest x1 0.03 us: per_device(): sub_cols = half_cols[:, data_index % 2].reshape(-1)]
  transfers between devices with their start and end apart: 3 -> 5, of which waited for: 2 -> 5; matrix products, arithmetic and copies ran while one was open for 25% -> 8% of each run, Pallas kernels for 0% -> 12%
where the time goes in v1:
time: 334 us; the launch traced here: 333 us
  waiting for transfers between devices  238 us (71%)
  Pallas kernels  40.8 us (12%)
  local copies, waits for them, and re-layouts  32.2 us (10%)
  between operations  13.9 us (4%)
  other arithmetic  6.77 us (2%)
    reduce_scatter x1, waiting for transfers between devices, per_device(): lax.psum_scatter(partial, 'dp', scatter_dimension=0, axis_index_groups=gr...  97.8 us
    all_gather x1, waiting for transfers between devices, per_device(): all_weights = lax.all_gather(w_pairs, 'dp', axis=0, tiled=True)  86.1 us
    ppermute x1, waiting for transfers between devices, per_device(): came = lax.ppermute(half_t, 'dp', swap)  45.4 us
    pallas_call x1, Pallas kernels, input_grad(): pl.pallas_call(input_grad_kernel, out_shape=jax.ShapeDtypeStruct(g.shape,...  24.3 us
    pallas_call x1, Pallas kernels, block_grads(): pl.pallas_call(functools.partial(block_grad_kernel, scale), out_shape=jax...  16.5 us
    unnamed x11, local copies, waits for them, and re-layouts  8.66 us
    reduce_scatter x1, waiting for transfers between devices, per_device(): ga_t = lax.psum_scatter(total_t, 'own', scatter_dimension=0, tiled=True)  7.72 us
    reshape x2, local copies, waits for them, and re-layouts, per_device(): weight_blocks.reshape(local_blocks // 2, 2, BLOCK, BLOCK)  7.37 us
  transfers between devices with their start and end apart: 5, of which 5 were waited for; matrix products, arithmetic and copies ran while one was open for 8% of the time, Pallas kernels for 12%

profile of v1, /device:TPU:9, one launch (start us, length us, event | category | flops | bytes accessed | tf_op | source)
XLA Modules:
  0.0 332.9 jit_solution(4785691084082897647)
XLA Ops:
  7.2 0.0 all-gather.3.cloned.1.call-start
  7.2 3.2 copy.13
  10.4 4.1 %copy.12 = bf16[128,8192]{0,1:T(8,128)(2,1)} copy(bf16[128,8192]{1,0:T(8,128)(2,1)} %param.5) | data formatting | bytes 4194304 | tf_op args[0]
  14.6 1.4 fusion.2
  15.9 0.0 copy-start.1
  15.9 1.3 collective-permute-start
  17.2 45.4 %collective-permute-done = bf16[2,4096,128]{2,1,0:T(8,128)(2,1)} collective-permute-done((bf16[2,4096,128]{2,1,0:T(8,128)(2,1)S(1)}, bf16[2,4096,128]{2,1,0:T(8,128)(2,1)}, u32[]{:S(2)}, u32[]{:S(2)}) %collective-permute-start) | collective-permute-done | bytes 2097184 | tf_op jit(solution)/shard_map/ppermute | solution.py:128
  62.6 0.0 all-gather.3.cloned.1.call-update
  62.6 0.0 all-gather.5.cloned.1.call-start
  62.7 0.0 copy-done.1
  62.7 3.0 reshape.30
  65.7 4.4 %copy.18 = bf16[52,2,64,64]{3,1,2,0:T(2,128)(2,1)} copy(bf16[52,2,64,64]{3,2,1,0:T(8,128)(2,1)} %reshape.30) | data formatting | bytes 1703936 | tf_op jit(solution)/shard_map/reshape | solution.py:116
  70.1 0.0 copy-start.2
  70.1 0.0 copy-start.3
  70.1 4.1 %reshape.31 = bf16[52,64,128]{2,1,0:T(8,128)(2,1)} reshape(bf16[52,64,2,64]{3,2,1,0:T(2,128)(2,1)} %bitcast.26) | data formatting | bytes 1703936 | tf_op jit(solution)/shard_map/reshape | solution.py:118
  74.2 0.0 all-gather.5.cloned.1.call-update
  74.2 0.0 reduce-scatter.3.cloned.1.call-start
  74.3 0.0 copy-done.2
  74.3 0.1 reshape.26
  74.4 0.1 reshape_squeeze.12.rows_ref
  74.5 0.0 copy-done.3
  74.5 0.1 reshape.27
  74.7 0.1 reshape_squeeze.13.rows_ref
  74.7 0.1 reshape_squeeze.14.cols_ref
  74.8 2.1 fusion
  76.9 1.6 slice_bitcast_fusion.1
  78.5 0.7 all-gather.3.cloned.1.call-done
  79.2 3.8 %slice_bitcast_fusion = (bf16[8192,128]{1,0:T(8,128)(2,1)}, bf16[8192,128]{1,0:T(8,128)(2,1)S(1)}) fusion(bf16[2,8192,128]{2,1,0:T(8,128)(2,1)} %all-gather.3.cloned.1.call-done), kind=kLoop, calls=%fused_computation.6 | loop fusion | bytes 8388608 | tf_op jit(solution)/shard_map/squeeze | solution.py:139
  83.0 16.5 %block_grads.1 = f32[208,64,128]{2,1,0:T(8,128)} custom-call(s32[416]{0:T(512)S(1)} %reshape_squeeze.13.rows_ref, s32[416]{0:T(512)S(1)} %reshape_squeeze.14.cols_ref, bf16[8192,128]{1,0:T(8,128)(2,1)S(1)} %get-tuple-element.13.a0, bf16[8192,128]{1,0:T(8,128)(2,1)S(1)} %get-tuple-element.11.a1, bf16[8192,128]{1,0:T(8,128)(2,1)} %get-tuple-element.12.g0.g_ref, ...), custom_call_target="tpu_custom_call" | custom-call | flops 3489660928 | bytes 16777216 | tf_op jit(solution)/shard_map/block_grads/pallas_call | solution.py:41
  99.5 0.0 copy-start
  99.5 0.0 reduce-scatter.3.cloned.1.call-update
  99.5 0.0 reduce-scatter.5.cloned.1.call-start
  99.6 0.1 reshape_squeeze.15.cols_ref
  99.7 86.1 %all-gather.5.cloned.1.call-done.w_ref = bf16[416,64,128]{2,1,0:T(8,128)(2,1)} async-done(((bf16[52,64,128]{2,1,0:T(8,128)(2,1)}), bf16[416,64,128]{2,1,0:T(8,128)(2,1)}) %all-gather.5.cloned.1.call-update) | async-done | bytes 6815760 | tf_op jit(solution)/shard_map/all_gather | solution.py:120
  185.7 0.0 copy-done
  185.7 24.3 %input_grad.1 = f32[8192,128]{1,0:T(8,128)} custom-call(s32[832]{0:T(1024)S(1)} %reshape_squeeze.12.rows_ref, s32[832]{0:T(1024)S(1)} %reshape_squeeze.15.cols_ref, bf16[416,64,128]{2,1,0:T(8,128)(2,1)} %all-gather.5.cloned.1.call-done.w_ref, bf16[8192,128]{1,0:T(8,128)(2,1)S(1)} %copy-done), custom_call_target="tpu_custom_call" | custom-call | flops 13958643712 | bytes 13631488 | tf_op jit(solution)/shard_map/input_grad/pallas_call | solution.py:87
  210.1 0.0 reduce-scatter.5.cloned.1.call-update
  210.1 97.8 %reduce-scatter.3.cloned.1.call-done = f32[52,64,128]{2,1,0:T(8,128)} async-done(((f32[208,64,128]{2,1,0:T(8,128)}), f32[52,64,128]{2,1,0:T(8,128)}) %reduce-scatter.3.cloned.1.call-update) | async-done | bytes 1703952 | tf_op jit(solution)/shard_map/reduce_scatter | solution.py:143
  307.9 1.6 convert_element_type.6
  309.5 0.8 reshape.28
  310.3 1.7 copy.14
  312.0 3.6 %reshape.29 = bf16[104,4096]{1,0:T(8,128)(2,1)} reshape(bf16[52,2,64,64]{3,2,1,0:T(8,128)(2,1)} %copy.14) | data formatting | bytes 1703936 | tf_op jit(solution)/shard_map/reshape | solution.py:150
  315.6 7.7 %reduce-scatter.5.cloned.1.call-done = f32[4096,128]{1,0:T(8,128)} async-done(((f32[8192,128]{1,0:T(8,128)}), f32[4096,128]{1,0:T(8,128)}) %reduce-scatter.5.cloned.1.call-update) | async-done | bytes 2097168 | tf_op jit(solution)/shard_map/reduce_scatter | solution.py:154
  323.3 1.7 convert_bitcast_fusion
  325.0 1.3 copy.16
  (3 shorter events, 0.1 us)
Async XLA Ops:
  7.2 72.0 %all-gather.3.cloned.1.call-start = ((), (), s32[]{:S(2)}) async-start(), calls=%async_computation.2 | async-start | bytes 6291456 | tf_op jit(solution)/shard_map/all_gather | solution.py:129
  15.9 46.8 %copy-start.1 = (bf16[104,4096]{1,0:T(8,128)(2,1)S(1)}, bf16[104,4096]{1,0:T(8,128)(2,1)}, u32[]{:S(2)}) copy-start(bf16[104,4096]{1,0:T(8,128)(2,1)} %param.7) | copy-start | bytes 2555908
  15.9 46.7 %collective-permute-start = (bf16[2,4096,128]{2,1,0:T(8,128)(2,1)S(1)}, bf16[2,4096,128]{2,1,0:T(8,128)(2,1)}, u32[]{:S(2)}, u32[]{:S(2)}) collective-permute-start(bf16[2,4096,128]{2,1,0:T(8,128)(2,1)S(1)} %fusion.2), channel_id=1, source_target_pairs={{0,2},{2,0},{4,6},{6,4},{8,10},{10,8},{12,14},{14,12},{1,3},{3,1},... | collective-permute-start | bytes 6291464 | tf_op jit(solution)/shard_map/ppermute | solution.py:128
  62.6 123.1 %all-gather.5.cloned.1.call-start = ((), (), s32[]{:S(2)}) async-start(), calls=%async_computation.4 | async-start | bytes 7667712 | tf_op jit(solution)/shard_map/all_gather | solution.py:120
  70.1 4.2 %copy-start.2 = (s32[1664]{0:T(1024)S(1)}, s32[1664]{0:T(1024)}, u32[]{:S(2)}) copy-start(s32[1664]{0:T(1024)} %param.8) | copy-start | bytes 19972
  70.1 4.5 %copy-start.3 = (s32[1664]{0:T(1024)S(1)}, s32[1664]{0:T(1024)}, u32[]{:S(2)}) copy-start(s32[1664]{0:T(1024)} %param.9) | copy-start | bytes 19972
  74.2 233.7 %reduce-scatter.3.cloned.1.call-start = ((), (), s32[]{:S(2)}) async-start(), calls=%async_computation.3 | async-start | bytes 8519680 | tf_op jit(solution)/shard_map/reduce_scatter | solution.py:143
  99.5 86.3 %copy-start = (bf16[8192,128]{1,0:T(8,128)(2,1)S(1)}, bf16[8192,128]{1,0:T(8,128)(2,1)}, u32[]{:S(2)}) copy-start(bf16[8192,128]{1,0:T(8,128)(2,1)} %get-tuple-element.12.g0.g_ref) | copy-start | bytes 6291460
  99.5 223.8 %reduce-scatter.5.cloned.1.call-start = ((), (), s32[]{:S(2)}) async-start(), calls=%async_computation.5 | async-start | bytes 6291456 | tf_op jit(solution)/shard_map/reduce_scatter | solution.py:154
Sparse Core Ops, SparseCore 0:
  62.7 16.4 all-gather.2
  82.0 103.7 all-gather.4
  188.0 119.8 reduce-scatter.2
  310.1 13.2 reduce-scatter.4

commit v2 on v1

--- a/solution.py
+++ b/solution.py
@@ -13,46 +13,205 @@
 MIB = 1024 * 1024
 
 
-def block_grad_kernel(scale, rows_ref, cols_ref, a0, a1, g0, g1, out_ref):
-    pairs = out_ref.shape[0]
-    start = pl.program_id(0) * pairs
+LEVELS = 32767.0
+SMALLEST = 1e-33
+CHUNKS = 4
+MESH = pl.DeviceIdType.MESH
+
+
+def block_grad_kernel(
+    scale,
+    owners,
+    rows_ref,
+    cols_ref,
+    a0,
+    g0,
+    out_ref,
+    a1,
+    g1,
+    sent,
+    sent_unit,
+    came,
+    came_unit,
+    kept,
+    over_sems,
+    side_sems,
+    word_sems,
+    unit_sems,
+):
+    dp, own = lax.axis_index("dp"), lax.axis_index("own")
+    n_data = 2 * owners
+    pair = dp + 1 - 2 * lax.rem(dp, 2)
+    each = out_ref.shape[0]
+    half = a0.shape[0] // 2
+    part = half // CHUNKS
     left_half = lax.broadcasted_iota(jnp.int32, (BLOCK, LANES), 1) < BLOCK
 
+    barrier = pltpu.get_barrier_semaphore()
+    pl.semaphore_signal(barrier, inc=1, device_id={"dp": pair}, device_id_type=MESH)
+    pl.semaphore_signal(barrier, inc=1, device_id={"own": 1 - own}, device_id_type=MESH)
+    for k in range(1, owners):
+        pl.semaphore_signal(
+            barrier,
+            inc=1,
+            device_id={"dp": lax.rem(dp + 2 * k, n_data)},
+            device_id_type=MESH,
+        )
+    pl.semaphore_wait(barrier, owners + 1)
+
+    def over(which, c):
+        rows = pl.ds(own * half + c * part, part)
+        return pltpu.make_async_remote_copy(
+            src_ref=(a0, g0)[which].at[rows],
+            dst_ref=(a1, g1)[which].at[rows],
+            send_sem=over_sems.at[0, which, c],
+            recv_sem=over_sems.at[1, which, c],
+            device_id={"dp": pair},
+            device_id_type=MESH,
+        )
+
+    def side(which, c):
+        rows = pl.ds(own * half + c * part, part)
+        target = (a1, g1)[which].at[rows]
+        return pltpu.make_async_remote_copy(
+            src_ref=target,
+            dst_ref=target,
+            send_sem=side_sems.at[0, which, c],
+            recv_sem=side_sems.at[1, which, c],
+            device_id={"own": 1 - own},
+            device_id_type=MESH,
+        )
+
+    order = [(which, c) for c in range(CHUNKS) for which in range(2)]
+    for which, c in order:
+        over(which, c).start()
+    for which, c in order:
+        over(which, c).wait_recv()
+        side(which, c).start()
+    for which, c in order:
+        side(which, c).wait_recv()
+
     def features(ref, other, at):
-        rows = pl.ds(pl.multiple_of(at * BLOCK, BLOCK), BLOCK)
-        return jnp.concatenate([ref[rows, :], other[rows, :]], axis=1)
-
-    def one_pair(p, carry):
-        b = 2 * (start + p)
+        return jnp.concatenate([ref[at], other[at]], axis=1)
+
+    def pair_sum(p):
+        b = 2 * p
         lhs = jnp.concatenate([features(a0, a1, rows_ref[b + k]) for k in range(2)], axis=0)
         rhs = jnp.concatenate([features(g0, g1, cols_ref[b + k]) for k in range(2)], axis=0)
         prod = lax.dot_general(
             lhs, rhs, (((1,), (1,)), ((), ())), preferred_element_type=jnp.float32
         )
-        out_ref[p] = jnp.where(left_half, prod[:BLOCK], prod[BLOCK:]) * scale
-        return carry
-
-    lax.fori_loop(0, pairs, one_pair, 0, unroll=4)
-
-
-def block_grads(rows, cols, a0, a1, g0, g1, scale, steps):
-    pairs = rows.shape[0] // 2
-    whole = pl.BlockSpec(a0.shape, lambda i, *_: (0, 0))
+        return jnp.where(left_half, prod[:BLOCK], prod[BLOCK:]) * scale
+
+    def words(k):
+        return pltpu.make_async_remote_copy(
+            src_ref=sent.at[k - 1],
+            dst_ref=came.at[k - 1],
+            send_sem=word_sems.at[0, k - 1],
+            recv_sem=word_sems.at[1, k - 1],
+            device_id={"dp": lax.rem(dp + 2 * k, n_data)},
+            device_id_type=MESH,
+        )
+
+    def steps(k):
+        return pltpu.make_async_remote_copy(
+            src_ref=sent_unit.at[k - 1],
+            dst_ref=came_unit.at[k - 1],
+            send_sem=unit_sems.at[0, k - 1],
+            recv_sem=unit_sems.at[1, k - 1],
+            device_id={"dp": lax.rem(dp + 2 * k, n_data)},
+            device_id_type=MESH,
+        )
+
+    def send_one(k, carry):
+        def pack(p, inner):
+            total = pair_sum(k * each + p)
+            peak = jnp.maximum(jnp.max(jnp.abs(total), axis=0, keepdims=True), SMALLEST)
+            levels = jnp.floor(total * (LEVELS / peak) + 0.5).astype(jnp.int32)
+            levels = jnp.clip(levels, -32767, 32767)
+            sent[k - 1, p] = levels[: BLOCK // 2] * 65536 + levels[BLOCK // 2 :]
+            sent_unit[k - 1, pl.ds(p, 1), :] = peak * (1.0 / LEVELS)
+            return inner
+
+        lax.fori_loop(0, each, pack, 0, unroll=4)
+        words(k).start()
+        steps(k).start()
+        return carry
+
+    lax.fori_loop(1, owners, send_one, 0)
+
+    def keep(p, carry):
+        kept[p] = pair_sum(p)
+        return carry
+
+    lax.fori_loop(0, each, keep, 0, unroll=4)
+
+    def wait_one(k, carry):
+        words(k).wait_recv()
+        steps(k).wait_recv()
+        return carry
+
+    lax.fori_loop(1, owners, wait_one, 0)
+
+    def add(p, carry):
+        top = kept[p, : BLOCK // 2]
+        low = kept[p, BLOCK // 2 :]
+        for k in range(owners - 1):
+            word = came[k, p]
+            unit = came_unit[k, pl.ds(p, 1), :]
+            low_levels = lax.shift_right_arithmetic(lax.shift_left(word, 16), 16)
+            top_levels = lax.shift_right_arithmetic(word - low_levels, 16)
+            top = top + top_levels.astype(jnp.float32) * unit
+            low = low + low_levels.astype(jnp.float32) * unit
+        out_ref[p] = jnp.concatenate([top, low], axis=0).astype(jnp.bfloat16)
+        return carry
+
+    lax.fori_loop(0, each, add, 0, unroll=2)
+
+    for which, c in order:
+        over(which, c).wait_send()
+        side(which, c).wait_send()
+
+    def sent_one(k, carry):
+        words(k).wait_send()
+        steps(k).wait_send()
+        return carry
+
+    lax.fori_loop(1, owners, sent_one, 0)
+
+
+def block_grads(rows, cols, a0, g0, scale, owners):
+    a0, g0 = (x.reshape(-1, BLOCK, x.shape[1]) for x in (a0, g0))
+    each = rows.shape[0] // 2 // owners
+    padded = -(-each // 8) * 8
+    smem = pl.BlockSpec(memory_space=pltpu.SMEM)
+    vmem = pl.BlockSpec(memory_space=pltpu.VMEM)
     return pl.pallas_call(
-        functools.partial(block_grad_kernel, scale),
-        out_shape=jax.ShapeDtypeStruct((pairs, BLOCK, LANES), jnp.float32),
-        grid_spec=pltpu.PrefetchScalarGridSpec(
-            num_scalar_prefetch=2,
-            grid=(steps,),
-            in_specs=[whole] * 4,
-            out_specs=pl.BlockSpec((pairs // steps, BLOCK, LANES), lambda i, *_: (i, 0, 0)),
+        functools.partial(block_grad_kernel, scale, owners),
+        out_shape=jax.ShapeDtypeStruct((each, BLOCK, LANES), jnp.bfloat16),
+        in_specs=[smem, smem, vmem, vmem],
+        out_specs=vmem,
+        scratch_shapes=[
+            pltpu.VMEM(a0.shape, a0.dtype),
+            pltpu.VMEM(g0.shape, g0.dtype),
+            pltpu.VMEM((owners - 1, each, BLOCK // 2, LANES), jnp.int32),
+            pltpu.VMEM((owners - 1, padded, LANES), jnp.float32),
+            pltpu.VMEM((owners - 1, each, BLOCK // 2, LANES), jnp.int32),
+            pltpu.VMEM((owners - 1, padded, LANES), jnp.float32),
+            pltpu.VMEM((each, BLOCK, LANES), jnp.float32),
+            pltpu.SemaphoreType.DMA((2, 2, CHUNKS)),
+            pltpu.SemaphoreType.DMA((2, 2, CHUNKS)),
+            pltpu.SemaphoreType.DMA((2, owners - 1)),
+            pltpu.SemaphoreType.DMA((2, owners - 1)),
+        ],
+        compiler_params=pltpu.CompilerParams(
+            vmem_limit_bytes=48 * MIB, collective_id=0, has_side_effects=True
         ),
-        compiler_params=pltpu.CompilerParams(vmem_limit_bytes=48 * MIB),
         cost_estimate=pl.CostEstimate(
-            flops=pairs * 2 * LANES * LANES * 512, bytes_accessed=16 * MIB, transcendentals=0
+            flops=100_000_000_000, bytes_accessed=16 * MIB, transcendentals=0
         ),
         name="block_grads",
-    )(rows, cols, a0, a1, g0, g1)
+    )(rows, cols, a0, g0)
 
 
 def input_grad_kernel(rows_ref, cols_ref, w_ref, g_ref, out_ref):
@@ -118,39 +277,29 @@
         .reshape(local_blocks // 2, BLOCK, LANES)
     )
     all_weights = lax.all_gather(w_pairs, "dp", axis=0, tiled=True)
-
-    half = width // 2
-    both = jnp.stack([acts, grad_out])
-    both_half = lax.dynamic_slice_in_dim(both, own_index * half, half, axis=2)
-    mine_t = both.transpose(0, 2, 1)
-    half_t = both_half.transpose(0, 2, 1)
-    swap = [(d, d ^ 1) for d in range(n_data)]
-    came = lax.ppermute(half_t, "dp", swap)
-    pair_t = lax.all_gather(came, "own", axis=1, tiled=True)
-
-    by_owner_rows = block_rows.reshape(n_data // 2, 2, 2, local_blocks)
-    by_owner_cols = block_cols.reshape(n_data // 2, 2, 2, local_blocks)
+    acts_t, grad_t = acts.T, grad_out.T
+    acts_t, w_pairs = lax.optimization_barrier((acts_t, w_pairs))
+
+    owners = n_data // 2
+    by_owner_rows = block_rows.reshape(owners, 2, 2, local_blocks)
+    by_owner_cols = block_cols.reshape(owners, 2, 2, local_blocks)
     half_rows = by_owner_rows[:, :, own_index]
     half_cols = by_owner_cols[:, :, own_index]
-    sub_rows = half_rows[:, data_index % 2].reshape(-1)
-    sub_cols = half_cols[:, data_index % 2].reshape(-1)
-
-    partial = block_grads(
-        sub_rows, sub_cols, mine_t[0], pair_t[0], mine_t[1], pair_t[1], scale, 4
-    )
-    later_rows, partial = lax.optimization_barrier((half_rows.reshape(-1), partial))
-    groups = [list(range(k, n_data, 2)) for k in range(2)]
-    summed = lax.psum_scatter(
-        partial, "dp", scatter_dimension=0, axis_index_groups=groups, tiled=True
-    )
+
+    def from_here(table):
+        ours = jnp.roll(table[:, data_index % 2], -(data_index // 2), axis=0)
+        return ours.reshape(-1)
+
+    sums = block_grads(
+        from_here(half_rows), from_here(half_cols), acts_t, grad_t, scale, owners
+    )
+    later_rows, sums = lax.optimization_barrier((half_rows.reshape(-1), sums))
     grad_blocks = (
-        summed.astype(jnp.bfloat16)
-        .reshape(local_blocks // 2, BLOCK, 2, BLOCK)
+        sums.reshape(local_blocks // 2, BLOCK, 2, BLOCK)
         .transpose(0, 2, 1, 3)
         .reshape(local_blocks, BLOCK * BLOCK)
     )
-
-    total_t = input_grad(later_rows, half_cols.reshape(-1), all_weights, mine_t[1], 8)
+    total_t = input_grad(later_rows, half_cols.reshape(-1), all_weights, grad_t, 8)
     ga_t = lax.psum_scatter(total_t, "own", scatter_dimension=0, tiled=True)
     grad_acts = ga_t.astype(jnp.bfloat16).T
     return (grad_blocks, grad_acts)

time: 334 us -> 252 us (0.75)
  waiting for transfers between devices: 238 us -> 8.25 us
  Pallas kernels: 40.8 us -> 206 us
  local copies, waits for them, and re-layouts: 32.2 us -> 20.5 us
  other arithmetic: 6.77 us -> 1.71 us
    pallas_call x1, Pallas kernels: 16.5 us -> 182 us  [block_grads(): pl.pallas_call(functools.partial(block_grad_kernel, scale, owners), out_s...]
    reduce_scatter x1 -> x0, waiting for transfers between devices: 97.8 us -> none  [per_device(): lax.psum_scatter(partial, 'dp', scatter_dimension=0, axis_index_groups=gr...]
    all_gather x1, waiting for transfers between devices: 86.1 us -> 0.01 us  [per_device(): all_weights = lax.all_gather(w_pairs, 'dp', axis=0, tiled=True)]
    ppermute x1 -> x0, waiting for transfers between devices: 45.4 us -> none  [per_device(): came = lax.ppermute(half_t, 'dp', swap)]
    squeeze x2 -> x0, local copies, waits for them, and re-layouts: 5.37 us -> none  [the longest x1 3.79 us: per_device(): pair_t[1]]
    optimization_barrier x0 -> x1, local copies, waits for them, and re-layouts: none -> 4.13 us  [per_device(): acts_t, w_pairs = lax.optimization_barrier((acts_t, w_pairs))]
    transpose x2 -> x0, other arithmetic: 3.48 us -> none  [the longest x1 2.12 us: per_device(): mine_t = both.transpose(0, 2, 1)]
    unnamed x11 -> x8, local copies, waits for them, and re-layouts: 8.66 us -> 6.31 us
  transfers between devices with their start and end apart: 5 -> 2, of which waited for: 5 -> 1; matrix products, arithmetic and copies ran while one was open for 8% -> 5% of each run, Pallas kernels for 12% -> 72%
where the time goes in v2:
time: 252 us; the launch traced here: 251 us
  Pallas kernels  206 us (82%)
  local copies, waits for them, and re-layouts  20.5 us (8%)
  between operations  14.2 us (6%)
  waiting for transfers between devices  8.25 us (3%)
    pallas_call x1, Pallas kernels, block_grads(): pl.pallas_call(functools.partial(block_grad_kernel, scale, owners), out_s...  182 us
    pallas_call x1, Pallas kernels, input_grad(): pl.pallas_call(input_grad_kernel, out_shape=jax.ShapeDtypeStruct(g.shape,...  24.4 us
    reduce_scatter x1, waiting for transfers between devices, per_device(): ga_t = lax.psum_scatter(total_t, 'own', scatter_dimension=0, tiled=True)  8.21 us
    unnamed x8, local copies, waits for them, and re-layouts  6.31 us
  transfers between devices with their start and end apart: 2, of which 1 were waited for; matrix products, arithmetic and copies ran while one was open for 5% of the time, Pallas kernels for 72%

profile of v2, /device:TPU:9, one launch (start us, length us, event | category | flops | bytes accessed | tf_op | source)
XLA Modules:
  0.0 251.2 jit_solution(11174596009863410851)
XLA Ops:
  7.2 0.0 all-gather.2.cloned.1.call-start
  7.2 2.8 %reshape.42 = bf16[52,2,64,64]{3,2,1,0:T(8,128)(2,1)S(1)} reshape(bf16[104,4096]{1,0:T(8,128)(2,1)} %param.9) | data formatting | bytes 1703936 | tf_op jit(solution)/shard_map/reshape | solution.py:275
  10.0 1.8 copy.18
  11.7 0.0 copy-start.1
  11.8 0.0 copy-start.2
  11.8 1.5 reshape.43
  13.3 0.0 all-gather.2.cloned.1.call-update
  13.3 0.0 reduce-scatter.2.cloned.1.call-start
  13.4 0.0 copy-done.1
  13.4 0.1 reshape.38
  13.6 0.1 reshape_squeeze.6.rows_ref
  13.6 0.0 copy-done.2
  13.7 0.1 reshape.40
  13.8 0.1 reshape.39.rows_ref
  13.9 0.1 reshape.41.cols_ref
  14.0 4.1 %copy.13 = bf16[8192,128]{1,0:T(8,128)(2,1)} copy(bf16[8192,128]{0,1:T(8,128)(2,1)} %bitcast.20) | data formatting | bytes 4194304 | tf_op jit(solution)/shard_map/optimization_barrier | solution.py:281
  18.2 3.2 %copy.14 = bf16[128,8192]{0,1:T(8,128)(2,1)S(1)} copy(bf16[128,8192]{1,0:T(8,128)(2,1)} %param.8) | data formatting | bytes 4194304 | tf_op args[1]
  21.4 0.0 copy-start
  21.4 1.8 copy-done
  23.2 182.0 %block_grads.1 = bf16[52,64,128]{2,1,0:T(8,128)(2,1)S(1)} custom-call(s32[416]{0:T(512)S(1)} %reshape.39.rows_ref, s32[416]{0:T(512)S(1)} %reshape.41.cols_ref, bf16[128,64,128]{2,1,0:T(8,128)(2,1)S(1)} %bitcast.17, bf16[128,64,128]{2,1,0:T(8,128)(2,1)S(1)} %bitcast.15), custom_call_target="tpu_custom_call" | custom-call | flops 99999997952 | bytes 16777216 | tf_op jit(solution)/shard_map/block_grads/pallas_call | solution.py:189
  205.2 0.1 reshape_squeeze.7.cols_ref
  205.3 0.0 all-gather.2.cloned.1.call-done.w_ref
  205.3 24.4 %input_grad.1 = f32[8192,128]{1,0:T(8,128)} custom-call(s32[832]{0:T(1024)S(1)} %reshape_squeeze.6.rows_ref, s32[832]{0:T(1024)S(1)} %reshape_squeeze.7.cols_ref, bf16[416,64,128]{2,1,0:T(8,128)(2,1)} %all-gather.2.cloned.1.call-done.w_ref, bf16[8192,128]{1,0:T(8,128)(2,1)S(1)} %bitcast.16), custom_call_target="tpu_custom_call" | custom-call | flops 13958643712 | bytes 13631488 | tf_op jit(solution)/shard_map/input_grad/pallas_call | solution.py:246
  229.8 0.0 reduce-scatter.2.cloned.1.call-update
  229.8 0.8 reshape.46
  230.6 0.4 copy.15
  231.0 2.2 reshape.47
  233.2 8.2 %reduce-scatter.2.cloned.1.call-done = f32[4096,128]{1,0:T(8,128)} async-done(((f32[8192,128]{1,0:T(8,128)}), f32[4096,128]{1,0:T(8,128)}) %reduce-scatter.2.cloned.1.call-update) | async-done | bytes 2097168 | tf_op jit(solution)/shard_map/reduce_scatter | solution.py:303
  241.4 1.7 convert_bitcast_fusion
  243.1 1.3 copy.16
  (7 shorter events, 0.1 us)
Async XLA Ops:
  7.2 198.2 %all-gather.2.cloned.1.call-start = ((), (), s32[]{:S(2)}) async-start(), calls=%async_computation.1 | async-start | bytes 7667712 | tf_op jit(solution)/shard_map/all_gather | solution.py:279
  11.7 1.7 copy-start.1
  11.8 1.9 copy-start.2
  13.3 228.1 %reduce-scatter.2.cloned.1.call-start = ((), (), s32[]{:S(2)}) async-start(), calls=%async_computation.2 | async-start | bytes 6291456 | tf_op jit(solution)/shard_map/reduce_scatter | solution.py:303
  21.4 1.8 copy-start
Sparse Core Ops, SparseCore 0:
  13.5 145.1 all-gather.1
  229.9 11.4 reduce-scatter.1

commit v3 on v2

--- a/solution.py
+++ b/solution.py
@@ -16,6 +16,7 @@
 LEVELS = 32767.0
 SMALLEST = 1e-33
 CHUNKS = 4
+JOIN_CHUNKS = 4
 MESH = pl.DeviceIdType.MESH
 
 
@@ -263,6 +264,56 @@
     )(rows, cols, weights, g)
 
 
+def join_kernel(total_ref, out_ref, came, sems):
+    own = lax.axis_index("own")
+    barrier = pltpu.get_barrier_semaphore()
+    pl.semaphore_signal(barrier, inc=1, device_id={"own": 1 - own}, device_id_type=MESH)
+    pl.semaphore_wait(barrier, 1)
+    half = came.shape[0]
+    part = half // JOIN_CHUNKS
+
+    def rows(which, c):
+        return pl.ds(pl.multiple_of(which * half + c * part, part), part)
+
+    def give(c):
+        return pltpu.make_async_remote_copy(
+            src_ref=total_ref.at[rows(1 - own, c), :],
+            dst_ref=came.at[pl.ds(c * part, part), :],
+            send_sem=sems.at[0, c],
+            recv_sem=sems.at[1, c],
+            device_id={"own": 1 - own},
+            device_id_type=MESH,
+        )
+
+    for c in range(JOIN_CHUNKS):
+        give(c).start()
+    for c in range(JOIN_CHUNKS):
+        give(c).wait_recv()
+        both = total_ref[rows(own, c), :] + came[pl.ds(c * part, part), :]
+        out_ref[:, pl.ds(c * part, part)] = both.T.astype(jnp.bfloat16)
+    for c in range(JOIN_CHUNKS):
+        give(c).wait_send()
+
+
+def join_halves(total_t):
+    width, tok_rows = total_t.shape
+    vmem = pl.BlockSpec(memory_space=pltpu.VMEM)
+    return pl.pallas_call(
+        join_kernel,
+        out_shape=jax.ShapeDtypeStruct((tok_rows, width // 2), jnp.bfloat16),
+        in_specs=[vmem],
+        out_specs=vmem,
+        scratch_shapes=[
+            pltpu.VMEM((width // 2, tok_rows), jnp.float32),
+            pltpu.SemaphoreType.DMA((2, JOIN_CHUNKS)),
+        ],
+        compiler_params=pltpu.CompilerParams(
+            vmem_limit_bytes=48 * MIB, collective_id=1, has_side_effects=True
+        ),
+        name="join_halves",
+    )(total_t)
+
+
 def per_device(acts, grad_out, weight_blocks, block_rows, block_cols):
     tok_rows, width = acts.shape
     n_data = lax.axis_size("dp")
@@ -300,8 +351,7 @@
         .reshape(local_blocks, BLOCK * BLOCK)
     )
     total_t = input_grad(later_rows, half_cols.reshape(-1), all_weights, grad_t, 8)
-    ga_t = lax.psum_scatter(total_t, "own", scatter_dimension=0, tiled=True)
-    grad_acts = ga_t.astype(jnp.bfloat16).T
+    grad_acts = join_halves(total_t)
     return (grad_blocks, grad_acts)
 
 

time: 252 us -> 253 us (level)
  waiting for transfers between devices: 8.25 us -> 0.02 us
  local copies, waits for them, and re-layouts: 20.5 us -> 27.4 us
  Pallas kernels: 206 us -> 211 us
    reduce_scatter x1 -> x0, waiting for transfers between devices: 8.21 us -> none  [per_device(): ga_t = lax.psum_scatter(total_t, 'own', scatter_dimension=0, tiled=True)]
    pallas_call x0 -> x1, Pallas kernels: none -> 4.38 us  [join_halves(): pl.pallas_call(join_kernel, out_shape=jax.ShapeDtypeStruct((tok_rows, wid...]
    transpose x1, local copies, waits for them, and re-layouts: 0.44 us -> 3.16 us  [per_device(): grad_blocks = sums.reshape(local_blocks // 2, BLOCK, 2, BLOCK).transpose(...]
    unnamed x8 -> x10, local copies, waits for them, and re-layouts: 6.31 us -> 8.15 us
  transfers between devices with their start and end apart: 2 -> 1, of which waited for: 1 -> 0; matrix products, arithmetic and copies ran while one was open for 5% -> 7% of each run, Pallas kernels for 72% -> 72%
where the time goes in v3:
time: 253 us
  Pallas kernels  211 us (83%)
  local copies, waits for them, and re-layouts  27.4 us (11%)
  between operations  14.2 us (6%)
    pallas_call x1, Pallas kernels, block_grads(): pl.pallas_call(functools.partial(block_grad_kernel, scale, owners), out_s...  182 us
    pallas_call x1, Pallas kernels, input_grad(): pl.pallas_call(input_grad_kernel, out_shape=jax.ShapeDtypeStruct(g.shape,...  24.5 us
    unnamed x10, local copies, waits for them, and re-layouts  8.15 us
  transfers between devices with their start and end apart: 1, of which 0 were waited for; matrix products, arithmetic and copies ran while one was open for 7% of the time, Pallas kernels for 72%

profile of v3, /device:TPU:9, one launch (start us, length us, event | category | flops | bytes accessed | tf_op | source)
XLA Modules:
  0.0 252.7 jit_solution(10801022616464425689)
XLA Ops:
  7.2 0.0 all-gather.2.cloned.1.call-start
  7.2 2.8 %reshape.42 = bf16[52,2,64,64]{3,2,1,0:T(8,128)(2,1)S(1)} reshape(bf16[104,4096]{1,0:T(8,128)(2,1)} %param.9) | data formatting | bytes 1703936 | tf_op jit(solution)/shard_map/reshape | solution.py:326
  10.0 1.8 copy.16
  11.7 0.0 copy-start.2
  11.8 0.0 copy-start.3
  11.8 1.5 reshape.43
  13.3 0.0 all-gather.2.cloned.1.call-update
  13.4 0.0 copy-done.2
  13.4 0.1 reshape.38
  13.5 0.1 reshape_squeeze.6.rows_ref
  13.6 0.0 copy-done.3
  13.6 0.1 reshape.40
  13.8 0.1 reshape.39.rows_ref
  13.9 0.1 reshape.41.cols_ref
  14.0 4.1 %copy.12 = bf16[8192,128]{1,0:T(8,128)(2,1)} copy(bf16[8192,128]{0,1:T(8,128)(2,1)} %bitcast.18) | data formatting | bytes 4194304 | tf_op jit(solution)/shard_map/optimization_barrier | solution.py:332
  18.1 3.2 %copy.13 = bf16[128,8192]{0,1:T(8,128)(2,1)S(1)} copy(bf16[128,8192]{1,0:T(8,128)(2,1)} %param.8) | data formatting | bytes 4194304 | tf_op args[1]
  21.3 0.0 copy-start.1
  21.3 1.8 copy-done.1
  23.1 182.1 %block_grads.1 = bf16[52,64,128]{2,1,0:T(8,128)(2,1)S(1)} custom-call(s32[416]{0:T(512)S(1)} %reshape.39.rows_ref, s32[416]{0:T(512)S(1)} %reshape.41.cols_ref, bf16[128,64,128]{2,1,0:T(8,128)(2,1)S(1)} %bitcast.15, bf16[128,64,128]{2,1,0:T(8,128)(2,1)S(1)} %bitcast.13), custom_call_target="tpu_custom_call" | custom-call | flops 99999997952 | bytes 16777216 | tf_op jit(solution)/shard_map/block_grads/pallas_call | solution.py:190
  205.2 1.7 reshape.46
  206.9 3.2 %copy.14 = bf16[52,2,64,64]{3,2,1,0:T(8,128)(2,1)} copy(bf16[52,2,64,64]{3,1,2,0:T(2,128)(2,1)} %bitcast.17) | data formatting | bytes 1703936 | tf_op jit(solution)/shard_map/transpose | solution.py:350
  210.1 3.6 %reshape.47 = bf16[104,4096]{1,0:T(8,128)(2,1)} reshape(bf16[52,2,64,64]{3,2,1,0:T(8,128)(2,1)} %copy.14) | data formatting | bytes 1703936 | tf_op jit(solution)/shard_map/reshape | solution.py:351
  213.7 0.1 reshape_squeeze.7.cols_ref
  213.8 0.0 all-gather.2.cloned.1.call-done.w_ref
  213.8 24.5 %input_grad.1.total_ref = f32[8192,128]{1,0:T(8,128)} custom-call(s32[832]{0:T(1024)S(1)} %reshape_squeeze.6.rows_ref, s32[832]{0:T(1024)S(1)} %reshape_squeeze.7.cols_ref, bf16[416,64,128]{2,1,0:T(8,128)(2,1)} %all-gather.2.cloned.1.call-done.w_ref, bf16[8192,128]{1,0:T(8,128)(2,1)S(1)} %bitcast.14), custom_call_target="tpu_custom_call" | custom-call | flops 13958643712 | bytes 13631488 | tf_op jit(solution)/shard_map/input_grad/pallas_call | solution.py:247
  238.3 0.0 copy-start
  238.3 2.2 copy-done
  240.5 4.4 %join_halves.1 = bf16[128,4096]{1,0:T(8,128)(2,1)S(1)} custom-call(f32[8192,128]{1,0:T(8,128)S(1)} %copy-done), custom_call_target="tpu_custom_call" | custom-call | tf_op jit(solution)/shard_map/join_halves/pallas_call | solution.py:301
  244.9 1.0 copy.18
  (7 shorter events, 0.1 us)
Async XLA Ops:
  7.2 206.7 %all-gather.2.cloned.1.call-start = ((), (), s32[]{:S(2)}) async-start(), calls=%async_computation | async-start | bytes 7667712 | tf_op jit(solution)/shard_map/all_gather | solution.py:330
  11.7 1.6 copy-start.2
  11.8 1.8 copy-start.3
  21.3 1.8 copy-start.1
  238.3 2.2 copy-start
Sparse Core Ops, SparseCore 0:
  13.5 145.1 all-gather.1

commit v4 on v3

--- a/solution.py
+++ b/solution.py
@@ -20,45 +20,16 @@
 MESH = pl.DeviceIdType.MESH
 
 
-def block_grad_kernel(
-    scale,
-    owners,
-    rows_ref,
-    cols_ref,
-    a0,
-    g0,
-    out_ref,
-    a1,
-    g1,
-    sent,
-    sent_unit,
-    came,
-    came_unit,
-    kept,
-    over_sems,
-    side_sems,
-    word_sems,
-    unit_sems,
-):
+def exchange_kernel(a0, g0, a1, g1, over_sems, side_sems):
     dp, own = lax.axis_index("dp"), lax.axis_index("own")
-    n_data = 2 * owners
     pair = dp + 1 - 2 * lax.rem(dp, 2)
-    each = out_ref.shape[0]
     half = a0.shape[0] // 2
     part = half // CHUNKS
-    left_half = lax.broadcasted_iota(jnp.int32, (BLOCK, LANES), 1) < BLOCK
 
     barrier = pltpu.get_barrier_semaphore()
     pl.semaphore_signal(barrier, inc=1, device_id={"dp": pair}, device_id_type=MESH)
     pl.semaphore_signal(barrier, inc=1, device_id={"own": 1 - own}, device_id_type=MESH)
-    for k in range(1, owners):
-        pl.semaphore_signal(
-            barrier,
-            inc=1,
-            device_id={"dp": lax.rem(dp + 2 * k, n_data)},
-            device_id_type=MESH,
-        )
-    pl.semaphore_wait(barrier, owners + 1)
+    pl.semaphore_wait(barrier, 2)
 
     def over(which, c):
         rows = pl.ds(own * half + c * part, part)
@@ -91,6 +62,64 @@
         side(which, c).start()
     for which, c in order:
         side(which, c).wait_recv()
+    for which, c in order:
+        over(which, c).wait_send()
+        side(which, c).wait_send()
+
+
+def exchange(a0, g0):
+    vmem = pl.BlockSpec(memory_space=pltpu.VMEM)
+    return pl.pallas_call(
+        exchange_kernel,
+        out_shape=(
+            jax.ShapeDtypeStruct(a0.shape, a0.dtype),
+            jax.ShapeDtypeStruct(g0.shape, g0.dtype),
+        ),
+        in_specs=[vmem, vmem],
+        out_specs=(vmem, vmem),
+        scratch_shapes=[
+            pltpu.SemaphoreType.DMA((2, 2, CHUNKS)),
+            pltpu.SemaphoreType.DMA((2, 2, CHUNKS)),
+        ],
+        compiler_params=pltpu.CompilerParams(
+            vmem_limit_bytes=48 * MIB, collective_id=2, has_side_effects=True
+        ),
+        name="exchange",
+    )(a0, g0)
+
+
+def block_grad_kernel(
+    scale,
+    owners,
+    rows_ref,
+    cols_ref,
+    a0,
+    g0,
+    a1,
+    g1,
+    out_ref,
+    sent,
+    sent_unit,
+    came,
+    came_unit,
+    kept,
+    word_sems,
+    unit_sems,
+):
+    dp = lax.axis_index("dp")
+    n_data = 2 * owners
+    each = out_ref.shape[0]
+    left_half = lax.broadcasted_iota(jnp.int32, (BLOCK, LANES), 1) < BLOCK
+
+    barrier = pltpu.get_barrier_semaphore()
+    for k in range(1, owners):
+        pl.semaphore_signal(
+            barrier,
+            inc=1,
+            device_id={"dp": lax.rem(dp + 2 * k, n_data)},
+            device_id_type=MESH,
+        )
+    pl.semaphore_wait(barrier, owners - 1)
 
     def features(ref, other, at):
         return jnp.concatenate([ref[at], other[at]], axis=1)
@@ -169,10 +198,6 @@
 
     lax.fori_loop(0, each, add, 0, unroll=2)
 
-    for which, c in order:
-        over(which, c).wait_send()
-        side(which, c).wait_send()
-
     def sent_one(k, carry):
         words(k).wait_send()
         steps(k).wait_send()
@@ -181,8 +206,7 @@
     lax.fori_loop(1, owners, sent_one, 0)
 
 
-def block_grads(rows, cols, a0, g0, scale, owners):
-    a0, g0 = (x.reshape(-1, BLOCK, x.shape[1]) for x in (a0, g0))
+def block_grads(rows, cols, a0, g0, a1, g1, scale, owners):
     each = rows.shape[0] // 2 // owners
     padded = -(-each // 8) * 8
     smem = pl.BlockSpec(memory_space=pltpu.SMEM)
@@ -190,18 +214,14 @@
     return pl.pallas_call(
         functools.partial(block_grad_kernel, scale, owners),
         out_shape=jax.ShapeDtypeStruct((each, BLOCK, LANES), jnp.bfloat16),
-        in_specs=[smem, smem, vmem, vmem],
+        in_specs=[smem, smem, vmem, vmem, vmem, vmem],
         out_specs=vmem,
         scratch_shapes=[
-            pltpu.VMEM(a0.shape, a0.dtype),
-            pltpu.VMEM(g0.shape, g0.dtype),
             pltpu.VMEM((owners - 1, each, BLOCK // 2, LANES), jnp.int32),
             pltpu.VMEM((owners - 1, padded, LANES), jnp.float32),
             pltpu.VMEM((owners - 1, each, BLOCK // 2, LANES), jnp.int32),
             pltpu.VMEM((owners - 1, padded, LANES), jnp.float32),
             pltpu.VMEM((each, BLOCK, LANES), jnp.float32),
-            pltpu.SemaphoreType.DMA((2, 2, CHUNKS)),
-            pltpu.SemaphoreType.DMA((2, 2, CHUNKS)),
             pltpu.SemaphoreType.DMA((2, owners - 1)),
             pltpu.SemaphoreType.DMA((2, owners - 1)),
         ],
@@ -212,11 +232,11 @@
             flops=100_000_000_000, bytes_accessed=16 * MIB, transcendentals=0
         ),
         name="block_grads",
-    )(rows, cols, a0, g0)
+    )(rows, cols, a0, g0, a1, g1)
 
 
 def input_grad_kernel(rows_ref, cols_ref, w_ref, g_ref, out_ref):
-    pairs = w_ref.shape[0]
+    pairs = w_ref.shape[1]
     start = pl.program_id(0) * pairs
     lane = lax.broadcasted_iota(jnp.int32, (BLOCK, LANES), 1)
     first = (lane < BLOCK).astype(jnp.float32).astype(jnp.bfloat16)
@@ -231,7 +251,7 @@
 
     def one_pair(p, carry):
         b = 2 * (start + p)
-        w = w_ref[p]
+        w = jnp.concatenate([w_ref[0, p], w_ref[1, p]], axis=0)
         lhs = jnp.concatenate([w * first, w * second], axis=0)
         rhs = jnp.concatenate([g_ref[span(cols_ref[b + k]), :] for k in range(2)], axis=0)
         prod = jnp.dot(lhs, rhs, preferred_element_type=jnp.float32)
@@ -243,7 +263,7 @@
 
 
 def input_grad(rows, cols, weights, g, steps):
-    pairs = weights.shape[0]
+    pairs = weights.shape[1]
     return pl.pallas_call(
         input_grad_kernel,
         out_shape=jax.ShapeDtypeStruct(g.shape, jnp.float32),
@@ -251,7 +271,9 @@
             num_scalar_prefetch=2,
             grid=(steps,),
             in_specs=[
-                pl.BlockSpec((pairs // steps, BLOCK, LANES), lambda i, *_: (i, 0, 0)),
+                pl.BlockSpec(
+                    (2, pairs // steps, BLOCK // 2, LANES), lambda i, *_: (0, i, 0, 0)
+                ),
                 pl.BlockSpec(g.shape, lambda i, *_: (0, 0)),
             ],
             out_specs=pl.BlockSpec(g.shape, lambda i, *_: (0, 0)),
@@ -327,9 +349,17 @@
         .transpose(0, 2, 1, 3)
         .reshape(local_blocks // 2, BLOCK, LANES)
     )
-    all_weights = lax.all_gather(w_pairs, "dp", axis=0, tiled=True)
+    n_groups = lax.axis_size("groups")
+    side = lax.axis_index("groups") % 2
+    w_side = lax.dynamic_slice_in_dim(w_pairs, side * (BLOCK // 2), BLOCK // 2, axis=1)
+    w_half = lax.all_gather(w_side, "dp", axis=0, tiled=True)
     acts_t, grad_t = acts.T, grad_out.T
-    acts_t, w_pairs = lax.optimization_barrier((acts_t, w_pairs))
+    acts_t, w_side = lax.optimization_barrier((acts_t, w_side))
+    a0, g0 = (x.reshape(-1, BLOCK, tok_rows) for x in (acts_t, grad_t))
+    a1, g1 = exchange(a0, g0)
+    w_half, a1 = lax.optimization_barrier((w_half, a1))
+    partners = [[g, g + 1] for g in range(0, n_groups, 2)]
+    all_weights = lax.all_gather(w_half, "groups", axis_index_groups=partners)
 
     owners = n_data // 2
     by_owner_rows = block_rows.reshape(owners, 2, 2, local_blocks)
@@ -342,7 +372,7 @@
         return ours.reshape(-1)
 
     sums = block_grads(
-        from_here(half_rows), from_here(half_cols), acts_t, grad_t, scale, owners
+        from_here(half_rows), from_here(half_cols), a0, g0, a1, g1, scale, owners
     )
     later_rows, sums = lax.optimization_barrier((half_rows.reshape(-1), sums))
     grad_blocks = (

time: 253 us -> 235 us (0.929)
  Pallas kernels: 211 us -> 189 us
  local copies, waits for them, and re-layouts: 27.4 us -> 30.7 us
    pallas_call x1, Pallas kernels: 182 us -> 86.2 us  [block_grads(): pl.pallas_call(functools.partial(block_grad_kernel, scale, owners), out_s...]
    pallas_call x0 -> x1, Pallas kernels: none -> 74.4 us  [exchange(): pl.pallas_call(exchange_kernel, out_shape=(jax.ShapeDtypeStruct(a0.shape,...]
    unnamed x10 -> x18, local copies, waits for them, and re-layouts: 8.15 us -> 13.1 us
  transfers between devices with their start and end apart: 1 -> 2, of which waited for: 0 -> 1; matrix products, arithmetic and copies ran while one was open for 7% -> 7% of each run, Pallas kernels for 72% -> 68%
where the time goes in v4:
time: 235 us
  Pallas kernels  189 us (80%)
  local copies, waits for them, and re-layouts  30.7 us (13%)
  between operations  14.3 us (6%)
    pallas_call x1, Pallas kernels, block_grads(): pl.pallas_call(functools.partial(block_grad_kernel, scale, owners), out_s...  86.2 us
    pallas_call x1, Pallas kernels, exchange(): pl.pallas_call(exchange_kernel, out_shape=(jax.ShapeDtypeStruct(a0.shape,...  74.4 us
    pallas_call x1, Pallas kernels, input_grad(): pl.pallas_call(input_grad_kernel, out_shape=jax.ShapeDtypeStruct(g.shape,...  24.5 us
    unnamed x18, local copies, waits for them, and re-layouts  13.1 us
  transfers between devices with their start and end apart: 2, of which 1 were waited for; matrix products, arithmetic and copies ran while one was open for 7% of the time, Pallas kernels for 68%

profile of v4, /device:TPU:9, one launch (start us, length us, event | category | flops | bytes accessed | tf_op | source)
XLA Modules:
  0.0 234.7 jit_solution(11893945971867932128)
XLA Ops:
  7.2 0.0 all-gather.4.cloned.1.call-start
  7.2 2.8 %reshape.42 = bf16[52,2,64,64]{3,2,1,0:T(8,128)(2,1)S(1)} reshape(bf16[104,4096]{1,0:T(8,128)(2,1)} %param.9) | data formatting | bytes 1703936 | tf_op jit(solution)/shard_map/reshape | solution.py:348
  10.0 1.8 copy.16
  11.8 0.0 copy-start.6
  11.8 0.0 copy-start.7
  11.8 0.8 reshape.43
  12.6 0.8 constant_dynamic-slice_fusion.2
  13.4 0.0 all-gather.4.cloned.1.call-update
  13.4 0.0 all-gather.6.cloned.1.call-start
  13.5 0.0 copy-done.6
  13.5 0.1 reshape.38
  13.6 0.1 reshape_squeeze.6.rows_ref
  13.7 0.0 copy-done.7
  13.7 0.1 reshape.40
  13.9 0.1 reshape_squeeze.7.cols_ref
  14.0 0.1 reshape.39.rows_ref
  14.1 0.1 reshape.41.cols_ref
  14.2 0.0 copy-start.5
  14.2 4.2 %copy.13 = bf16[128,8192]{0,1:T(8,128)(2,1)} copy(bf16[128,8192]{1,0:T(8,128)(2,1)} %param.8) | data formatting | bytes 4194304 | tf_op args[1]
  18.4 0.0 copy-done.5
  18.4 2.4 %copy.12 = bf16[8192,128]{1,0:T(8,128)(2,1)} copy(bf16[8192,128]{0,1:T(8,128)(2,1)S(1)} %bitcast.21) | data formatting | bytes 4194304 | tf_op jit(solution)/shard_map/optimization_barrier | solution.py:357
  20.8 74.4 %exchange.1 = (bf16[128,64,128]{2,1,0:T(8,128)(2,1)S(1)}, bf16[128,64,128]{2,1,0:T(8,128)(2,1)S(1)}) custom-call(bf16[128,64,128]{2,1,0:T(8,128)(2,1)} %bitcast.17, bf16[128,64,128]{2,1,0:T(8,128)(2,1)} %bitcast.14), custom_call_target="tpu_custom_call" | custom-call | tf_op jit(solution)/shard_map/exchange/pallas_call | solution.py:72
  95.2 0.0 copy-start.3
  95.3 1.3 copy-done.3
  96.6 0.0 copy-start.4
  96.6 1.3 copy-done.4
  97.9 0.0 copy-start
  97.9 0.1 all-gather.4.cloned.1.call-done
  98.0 0.0 all-gather.6.cloned.1.call-update
  98.0 1.5 copy-done
  99.5 0.0 copy-start.1
  99.5 1.6 copy-done.1
  101.1 86.2 %block_grads.1 = bf16[52,64,128]{2,1,0:T(8,128)(2,1)S(1)} custom-call(s32[416]{0:T(512)S(1)} %reshape.39.rows_ref, s32[416]{0:T(512)S(1)} %reshape.41.cols_ref, bf16[128,64,128]{2,1,0:T(8,128)(2,1)S(1)} %bitcast.18, bf16[128,64,128]{2,1,0:T(8,128)(2,1)S(1)} %bitcast.15, bf16[128,64,128]{2,1,0:T(8,128)(2,1)} %copy-done.3, bf16[128,64,128]{2,1,0:T(8,128)(2,1)} %copy-done.4), custom_call_target="tpu_custom_call" | custom-call | flops 99999997952 | bytes 16777216 | tf_op jit(solution)/shard_map/block_grads/pallas_call | solution.py:214
  187.4 1.7 reshape.46
  189.0 3.2 %copy.14 = bf16[52,2,64,64]{3,2,1,0:T(8,128)(2,1)} copy(bf16[52,2,64,64]{3,1,2,0:T(2,128)(2,1)} %bitcast.20) | data formatting | bytes 1703936 | tf_op jit(solution)/shard_map/transpose | solution.py:380
  192.2 3.6 %reshape.47 = bf16[104,4096]{1,0:T(8,128)(2,1)} reshape(bf16[52,2,64,64]{3,2,1,0:T(8,128)(2,1)} %copy.14) | data formatting | bytes 1703936 | tf_op jit(solution)/shard_map/reshape | solution.py:381
  195.8 0.0 all-gather.6.cloned.1.call-done
  195.8 24.5 %input_grad.1.total_ref = f32[8192,128]{1,0:T(8,128)} custom-call(s32[832]{0:T(1024)S(1)} %reshape_squeeze.6.rows_ref, s32[832]{0:T(1024)S(1)} %reshape_squeeze.7.cols_ref, bf16[2,416,32,128]{3,2,1,0:T(8,128)(2,1)} %bitcast.24, bf16[8192,128]{1,0:T(8,128)(2,1)S(1)} %bitcast.16), custom_call_target="tpu_custom_call" | custom-call | flops 13958643712 | bytes 13631488 | tf_op jit(solution)/shard_map/input_grad/pallas_call | solution.py:267
  220.3 0.0 copy-start.2
  220.3 2.2 copy-done.2
  222.5 4.4 %join_halves.1 = bf16[128,4096]{1,0:T(8,128)(2,1)S(1)} custom-call(f32[8192,128]{1,0:T(8,128)S(1)} %copy-done.2), custom_call_target="tpu_custom_call" | custom-call | tf_op jit(solution)/shard_map/join_halves/pallas_call | solution.py:323
  226.9 1.0 copy.18
  (7 shorter events, 0.1 us)
Async XLA Ops:
  7.2 90.8 %all-gather.4.cloned.1.call-start = ((), (), s32[]{:S(2)}) async-start(), calls=%async_computation | async-start | bytes 3833856 | tf_op jit(solution)/shard_map/all_gather | solution.py:355
  11.8 1.7 copy-start.6
  11.8 1.9 copy-start.7
  13.4 182.4 %all-gather.6.cloned.1.call-start = ((), (), s32[]{:S(2)}) async-start(), calls=%async_computation.1 | async-start | bytes 10223616 | tf_op jit(solution)/shard_map/all_gather | solution.py:362
  14.2 4.2 %copy-start.5 = (bf16[128,8192]{1,0:T(8,128)(2,1)S(1)}, bf16[128,8192]{1,0:T(8,128)(2,1)}, u32[]{:S(2)}) copy-start(bf16[128,8192]{1,0:T(8,128)(2,1)} %param.7) | copy-start | bytes 6291460
  95.2 1.3 copy-start.3
  96.6 1.3 copy-start.4
  97.9 1.6 copy-start
  99.5 1.6 copy-start.1
  220.3 2.2 copy-start.2
Sparse Core Ops, SparseCore 0:
  13.5 84.4 all-gather.3
  99.5 85.7 all-gather.5

commit v5 on v4

--- a/solution.py
+++ b/solution.py
@@ -259,7 +259,7 @@
             out_ref[span(rows_ref[b + k]), :] += prod[k * BLOCK : (k + 1) * BLOCK]
         return carry
 
-    lax.fori_loop(0, pairs, one_pair, 0, unroll=4)
+    lax.fori_loop(0, pairs, one_pair, 0, unroll=13)
 
 
 def input_grad(rows, cols, weights, g, steps):

time: 235 us -> 225 us (0.957)
  Pallas kernels: 189 us -> 179 us
    pallas_call x1, Pallas kernels: 24.5 us -> 14.4 us  [input_grad(): pl.pallas_call(input_grad_kernel, out_shape=jax.ShapeDtypeStruct(g.shape,...]
  transfers between devices with their start and end apart: 2 -> 2, of which waited for: 1 -> 1; matrix products, arithmetic and copies ran while one was open for 7% -> 7% of each run, Pallas kernels for 68% -> 72%
where the time goes in v5:
time: 225 us
  Pallas kernels  179 us (80%)
  local copies, waits for them, and re-layouts  30.7 us (14%)
  between operations  14.3 us (6%)
    pallas_call x1, Pallas kernels, block_grads(): pl.pallas_call(functools.partial(block_grad_kernel, scale, owners), out_s...  86.2 us
    pallas_call x1, Pallas kernels, exchange(): pl.pallas_call(exchange_kernel, out_shape=(jax.ShapeDtypeStruct(a0.shape,...  74.4 us
    pallas_call x1, Pallas kernels, input_grad(): pl.pallas_call(input_grad_kernel, out_shape=jax.ShapeDtypeStruct(g.shape,...  14.4 us
    unnamed x18, local copies, waits for them, and re-layouts  13.1 us
    reshape x2, local copies, waits for them, and re-layouts, per_device(): weight_blocks.reshape(local_blocks // 2, 2, BLOCK, BLOCK)  4.52 us
  transfers between devices with their start and end apart: 2, of which 1 were waited for; matrix products, arithmetic and copies ran while one was open for 7% of the time, Pallas kernels for 72%

profile of v5, /device:TPU:9, one launch (start us, length us, event | category | flops | bytes accessed | tf_op | source)
XLA Modules:
  0.0 224.7 jit_solution(8853077415693615998)
XLA Ops:
  7.2 0.0 all-gather.4.cloned.1.call-start
  7.2 2.8 %reshape.42 = bf16[52,2,64,64]{3,2,1,0:T(8,128)(2,1)S(1)} reshape(bf16[104,4096]{1,0:T(8,128)(2,1)} %param.9) | data formatting | bytes 1703936 | tf_op jit(solution)/shard_map/reshape | solution.py:348
  10.0 1.8 copy.16
  11.8 0.0 copy-start.6
  11.8 0.0 copy-start.7
  11.8 0.8 reshape.43
  12.6 0.8 constant_dynamic-slice_fusion.2
  13.4 0.0 all-gather.4.cloned.1.call-update
  13.4 0.0 all-gather.6.cloned.1.call-start
  13.5 0.0 copy-done.6
  13.5 0.1 reshape.38
  13.6 0.1 reshape_squeeze.6.rows_ref
  13.7 0.0 copy-done.7
  13.7 0.1 reshape.40
  13.9 0.1 reshape_squeeze.7.cols_ref
  14.0 0.1 reshape.39.rows_ref
  14.1 0.1 reshape.41.cols_ref
  14.2 0.0 copy-start.5
  14.2 4.2 %copy.13 = bf16[128,8192]{0,1:T(8,128)(2,1)} copy(bf16[128,8192]{1,0:T(8,128)(2,1)} %param.8) | data formatting | bytes 4194304 | tf_op args[1]
  18.4 0.0 copy-done.5
  18.4 2.4 %copy.12 = bf16[8192,128]{1,0:T(8,128)(2,1)} copy(bf16[8192,128]{0,1:T(8,128)(2,1)S(1)} %bitcast.21) | data formatting | bytes 4194304 | tf_op jit(solution)/shard_map/optimization_barrier | solution.py:357
  20.8 74.4 %exchange.1 = (bf16[128,64,128]{2,1,0:T(8,128)(2,1)S(1)}, bf16[128,64,128]{2,1,0:T(8,128)(2,1)S(1)}) custom-call(bf16[128,64,128]{2,1,0:T(8,128)(2,1)} %bitcast.17, bf16[128,64,128]{2,1,0:T(8,128)(2,1)} %bitcast.14), custom_call_target="tpu_custom_call" | custom-call | tf_op jit(solution)/shard_map/exchange/pallas_call | solution.py:72
  95.2 0.0 copy-start.3
  95.3 1.3 copy-done.3
  96.6 0.0 copy-start.4
  96.6 1.3 copy-done.4
  97.9 0.0 copy-start
  97.9 0.1 all-gather.4.cloned.1.call-done
  98.0 0.0 all-gather.6.cloned.1.call-update
  98.0 1.5 copy-done
  99.5 0.0 copy-start.1
  99.5 1.6 copy-done.1
  101.1 86.2 %block_grads.1 = bf16[52,64,128]{2,1,0:T(8,128)(2,1)S(1)} custom-call(s32[416]{0:T(512)S(1)} %reshape.39.rows_ref, s32[416]{0:T(512)S(1)} %reshape.41.cols_ref, bf16[128,64,128]{2,1,0:T(8,128)(2,1)S(1)} %bitcast.18, bf16[128,64,128]{2,1,0:T(8,128)(2,1)S(1)} %bitcast.15, bf16[128,64,128]{2,1,0:T(8,128)(2,1)} %copy-done.3, bf16[128,64,128]{2,1,0:T(8,128)(2,1)} %copy-done.4), custom_call_target="tpu_custom_call" | custom-call | flops 99999997952 | bytes 16777216 | tf_op jit(solution)/shard_map/block_grads/pallas_call | solution.py:214
  187.4 1.7 reshape.46
  189.0 3.2 %copy.14 = bf16[52,2,64,64]{3,2,1,0:T(8,128)(2,1)} copy(bf16[52,2,64,64]{3,1,2,0:T(2,128)(2,1)} %bitcast.20) | data formatting | bytes 1703936 | tf_op jit(solution)/shard_map/transpose | solution.py:380
  192.2 3.6 %reshape.47 = bf16[104,4096]{1,0:T(8,128)(2,1)} reshape(bf16[52,2,64,64]{3,2,1,0:T(8,128)(2,1)} %copy.14) | data formatting | bytes 1703936 | tf_op jit(solution)/shard_map/reshape | solution.py:381
  195.8 0.0 all-gather.6.cloned.1.call-done
  195.8 14.4 %input_grad.1.total_ref = f32[8192,128]{1,0:T(8,128)} custom-call(s32[832]{0:T(1024)S(1)} %reshape_squeeze.6.rows_ref, s32[832]{0:T(1024)S(1)} %reshape_squeeze.7.cols_ref, bf16[2,416,32,128]{3,2,1,0:T(8,128)(2,1)} %bitcast.24, bf16[8192,128]{1,0:T(8,128)(2,1)S(1)} %bitcast.16), custom_call_target="tpu_custom_call" | custom-call | flops 13958643712 | bytes 13631488 | tf_op jit(solution)/shard_map/input_grad/pallas_call | solution.py:267
  210.3 0.0 copy-start.2
  210.3 2.2 copy-done.2
  212.5 4.4 %join_halves.1 = bf16[128,4096]{1,0:T(8,128)(2,1)S(1)} custom-call(f32[8192,128]{1,0:T(8,128)S(1)} %copy-done.2), custom_call_target="tpu_custom_call" | custom-call | tf_op jit(solution)/shard_map/join_halves/pallas_call | solution.py:323
  216.8 1.0 copy.18
  (7 shorter events, 0.1 us)
Async XLA Ops:
  7.2 90.8 %all-gather.4.cloned.1.call-start = ((), (), s32[]{:S(2)}) async-start(), calls=%async_computation | async-start | bytes 3833856 | tf_op jit(solution)/shard_map/all_gather | solution.py:355
  11.8 1.7 copy-start.6
  11.8 1.9 copy-start.7
  13.4 182.4 %all-gather.6.cloned.1.call-start = ((), (), s32[]{:S(2)}) async-start(), calls=%async_computation.1 | async-start | bytes 10223616 | tf_op jit(solution)/shard_map/all_gather | solution.py:362
  14.2 4.2 %copy-start.5 = (bf16[128,8192]{1,0:T(8,128)(2,1)S(1)}, bf16[128,8192]{1,0:T(8,128)(2,1)}, u32[]{:S(2)}) copy-start(bf16[128,8192]{1,0:T(8,128)(2,1)} %param.7) | copy-start | bytes 6291460
  95.2 1.3 copy-start.3
  96.6 1.3 copy-start.4
  97.9 1.6 copy-start
  99.5 1.6 copy-start.1
  210.3 2.2 copy-start.2
Sparse Core Ops, SparseCore 0:
  13.5 84.4 all-gather.3
  99.5 85.7 all-gather.5
